TPU v7x, 1024 devices: a whole 8x8x8 slice. The times are simulated.
1024 devices in a mesh: expert: 16 (over x, core), shard: 64 (over z, y).
Axes of the slice: x: 8, y: 8, z: 8, core: 2. Of those that a mesh axis runs over, the one named last changes fastest.
Arguments:
- tokens: bfloat16 [1536, 2080], P('shard', 'expert'), may hold values from -6 to 6
- out_grad: bfloat16 [1536, 2080], P('shard', 'expert'), may hold values from -6 to 6
- gate_probs: bfloat16 [1536], P('shard'), may hold values from 0.19921875 to 1
- expert_ids: int32 [1536], P('shard'), may hold values from 0 to 15
- slots: int32 [1536], P('shard'), may hold values from -1 to 2, as said below
- w_in: bfloat16 [16, 2080, 6144], P('expert', None, 'shard'), may hold values from -0.125 to 0.125
- w_out: bfloat16 [16, 6144, 2080], P('expert', 'shard'), may hold values from -0.078125 to 0.078125
Outputs:
- token_grad: bfloat16 [1536, 2080], P('shard', 'expert')
- w_in_grad: float32 [16, 2080, 6144], P('expert', None, 'shard')
- w_out_grad: float32 [16, 6144, 2080], P('expert', 'shard')
Inputs may be any that keep to these rules, and one draw needn't show every extreme that they name: `slots`: the token's place, counted from 0 in token order, among the tokens of its block of 24 that chose the same expert; -1 where that place is 3 or more (a dropped token).
All inputs are finite; a program needn't handle non-finite values.
Results may differ from a plain program's by a relative error of at most 0.0031.
Values may be sent and summed in bfloat16 or wider, within the bound.
A program may use at most 32 MiB of HBM per device.

v0:
```python
import jax
import jax.numpy as jnp
from jax import lax
from jax.sharding import PartitionSpec as P

CAP = 3


root_two_over_pi = 0.7978845608028654
cubic_coef = 0.044715


def gelu_parts(pre_act):
    inner = root_two_over_pi * (pre_act + cubic_coef * pre_act * pre_act * pre_act)
    tanh_val = jnp.tanh(inner)
    value = 0.5 * pre_act * (1.0 + tanh_val)
    slope = 0.5 * (1.0 + tanh_val) + 0.5 * pre_act * (
        1.0 - tanh_val * tanh_val
    ) * root_two_over_pi * (1.0 + 3.0 * cubic_coef * pre_act * pre_act)
    return (value, slope)


def inner_rows(left, right):
    return lax.dot_general(
        left, right, (((0,), (0,)), ((), ())), preferred_element_type=jnp.float32
    )


def local_grads(x_rows, g_rows, q_rows, w_first, w_second):
    pre_act = jnp.dot(x_rows, w_first, preferred_element_type=jnp.float32)
    back_grad = lax.dot_general(
        g_rows, w_second, (((1,), (1,)), ((), ())), preferred_element_type=jnp.float32
    )
    value, slope = gelu_parts(pre_act)
    gates = q_rows.astype(jnp.float32)[:, None]
    scaled = (gates * value).astype(jnp.bfloat16)
    dpre = (gates * back_grad * slope).astype(jnp.bfloat16)
    return (scaled, dpre)


def local(tokens, out_grad, gate_probs, expert_ids, slots, w_in, w_out):
    n_expert = lax.axis_size("expert")
    my_expert = lax.axis_index("expert")
    capacity = CAP
    tok_count, features = tokens.shape
    slot_key = jnp.where(slots >= 0, expert_ids * capacity + slots, -1)
    picker = (
        slot_key[None, :] == jnp.arange(n_expert * capacity, dtype=jnp.int32)[:, None]
    ).astype(jnp.bfloat16)
    x_send = jnp.dot(picker, tokens, preferred_element_type=jnp.float32).astype(jnp.bfloat16)
    g_send = jnp.dot(picker, out_grad, preferred_element_type=jnp.float32).astype(jnp.bfloat16)
    x_send = x_send.reshape(n_expert, capacity, features)
    g_send = g_send.reshape(n_expert, capacity, features)
    x_recv, g_recv = (
        lax.all_to_all(x_send, "expert", split_axis=0, concat_axis=2, tiled=True),
        lax.all_to_all(g_send, "expert", split_axis=0, concat_axis=2, tiled=True),
    )
    x_mine = x_recv.reshape(capacity, features * n_expert)
    g_mine = g_recv.reshape(capacity, features * n_expert)
    mine_sel = (
        slot_key[None, :] == (my_expert * capacity + jnp.arange(capacity, dtype=jnp.int32))[:, None]
    )
    gate_mine = jnp.sum(
        jnp.where(mine_sel, gate_probs.astype(jnp.float32)[None, :], 0.0), axis=1
    ).astype(jnp.bfloat16)
    w_first = w_in[0]
    w_second = w_out[0]
    x_all, g_all, q_all = (
        lax.all_gather(x_mine, "shard", axis=0, tiled=True),
        lax.all_gather(g_mine, "shard", axis=0, tiled=True),
        lax.all_gather(gate_mine, "shard", axis=0, tiled=True),
    )
    scaled, dpre_all = local_grads(x_all, g_all, q_all, w_first, w_second)
    w_out_g = inner_rows(scaled, g_all)
    w_in_g = inner_rows(x_all, dpre_all)
    all_terms = lax.dot_general(
        dpre_all, w_first, (((1,), (1,)), ((), ())), preferred_element_type=jnp.float32
    )
    mine_sum = lax.psum_scatter(all_terms, "shard", scatter_dimension=0, tiled=True)
    mine_grad = mine_sum.astype(jnp.bfloat16)
    came_back = lax.all_to_all(mine_grad, "expert", split_axis=1, concat_axis=0, tiled=True)
    branch = inner_rows(picker, came_back)
    token_grad = (out_grad.astype(jnp.float32) + branch).astype(jnp.bfloat16)
    return (token_grad, w_in_g[None], w_out_g[None])


def solution(mesh):
    placed = (
        P("shard", "expert"),
        P("shard", "expert"),
        P("shard"),
        P("shard"),
        P("shard"),
        P("expert", None, "shard"),
        P("expert", "shard", None),
    )
    return jax.shard_map(
        local,
        mesh=mesh,
        in_specs=placed,
        out_specs=(P("shard", "expert"), P("expert", None, "shard"), P("expert", "shard", None)),
        check_vma=False,
    )
```

profile of v0, /device:TPU:1, one launch (start us, length us, event | category | flops | bytes accessed | tf_op | source)
XLA Modules:
  0.0 597.3 jit_solution(17414479953780211627)
XLA Ops:
  0.6 0.7 compare_select_fusion
  1.4 0.8 convolution_convert_fusion
  2.2 0.7 reshape.48
  2.9 17.4 %all-to-all-start.1 = ((bf16[16,2,195]{2,1,0:T(2,128)(2,1)}), bf16[16,2,195]{2,1,0:T(2,128)(2,1)S(1)}, u32[]{:S(2)}, u32[]{:S(2)}) async-start(bf16[16,2,195]{2,1,0:T(2,128)(2,1)} %reshape.48), calls=%async_computation.1 | async-start | bytes 32768 | tf_op jit(solution)/shard_map/all_to_all | solution.py:55
  20.4 0.8 convolution_convert_fusion.1
  21.2 0.7 convert_element_type.32
  21.9 0.7 reshape.46
  22.6 5.2 all-to-all-done.1
  27.8 3.7 all-to-all-start
  31.6 1.4 fusion.25
  33.9 120.5 %all-reduce = bf16[192]{0:T(256)(128)(2,1)S(1)} all-reduce(bf16[192]{0:T(256)(128)(2,1)S(1)} %dynamic-update-slice), channel_id=1, replica_groups=mesh['expert'=16,'shard'=64] {'shard'}, use_global_device_ids=true, to_apply=%add | all-reduce | flops 192 | bytes 768
  155.6 36.3 %all-gather = bf16[64,3,2080]{2,1,0:T(4,128)(2,1)S(1)} all-gather(bf16[1,3,2080]{2,1,0:T(4,128)(2,1)S(1)} %reshape.37), channel_id=1, replica_groups=mesh['expert'=16,'shard'=64] {'shard'}, dimensions={0}, use_global_device_ids=true | all-gather | bytes 811200 | tf_op jit(solution)/shard_map/all_gather | solution.py:70
  191.9 0.7 reshape.38
  192.6 37.5 %all-gather.1 = bf16[64,3,2080]{2,1,0:T(4,128)(2,1)S(1)} all-gather(bf16[1,3,2080]{2,1,0:T(4,128)(2,1)S(1)} %reshape.39), channel_id=1, replica_groups=mesh['expert'=16,'shard'=64] {'shard'}, dimensions={0}, use_global_device_ids=true | all-gather | bytes 811200 | tf_op jit(solution)/shard_map/all_gather | solution.py:69
  230.2 0.7 reshape.40
  230.9 0.4 fusion.5
  231.3 1.3 convolution_bitcast_fusion
  233.3 242.5 %all-reduce.3 = bf16[192,2080]{1,0:T(8,128)(2,1)} all-reduce(f32[192,2080]{1,0:T(8,128)S(1)} %fusion.3), channel_id=2, replica_groups=mesh['expert'=16,'shard'=64] {'shard'}, use_global_device_ids=true, to_apply=%region_1.2.clone | all-reduce | flops 399360 | bytes 2396160
  475.9 0.9 dynamic-slice_convert_fusion
  477.0 0.7 reshape.50
  477.6 111.3 %all-to-all-start.2 = ((bf16[16,2,195]{2,1,0:T(2,128)(2,1)}), bf16[16,2,195]{2,1,0:T(2,128)(2,1)S(1)}, u32[]{:S(2)}, u32[]{:S(2)}) async-start(bf16[16,2,195]{2,1,0:T(2,128)(2,1)} %reshape.50), calls=%async_computation.2 | async-start | bytes 32768 | tf_op jit(solution)/shard_map/all_to_all | solution.py:81
  589.0 1.2 convolution_bitcast_fusion.1
  590.2 6.1 %all-to-all-done.2 = bf16[16,2,195]{2,1,0:T(2,128)(2,1)S(1)} async-done(((bf16[16,2,195]{2,1,0:T(2,128)(2,1)}), bf16[16,2,195]{2,1,0:T(2,128)(2,1)S(1)}, u32[]{:S(2)}, u32[]{:S(2)}) %all-to-all-start.2) | async-done | bytes 12512 | tf_op jit(solution)/shard_map/all_to_all | solution.py:81
  596.5 0.8 fusion.2
  (27 shorter events, 2.0 us)
Async XLA Ops:
  0.6 230.3 %copy-start = (bf16[1,2080,96]{1,2,0:T(8,128)(2,1)S(1)}, bf16[1,2080,96]{1,2,0:T(8,128)(2,1)}, u32[]{:S(2)}) copy-start(bf16[1,2080,96]{1,2,0:T(8,128)(2,1)} %param.12) | copy-start | bytes 1198084
  2.9 24.8 %all-to-all-start.1 = ((bf16[16,2,195]{2,1,0:T(2,128)(2,1)}), bf16[16,2,195]{2,1,0:T(2,128)(2,1)S(1)}, u32[]{:S(2)}, u32[]{:S(2)}) async-start(bf16[16,2,195]{2,1,0:T(2,128)(2,1)} %reshape.48), calls=%async_computation.1 | async-start | bytes 32768 | tf_op jit(solution)/shard_map/all_to_all | solution.py:55
  27.8 127.5 %all-to-all-start = ((bf16[16,2,195]{2,1,0:T(2,128)(2,1)}), bf16[16,2,195]{2,1,0:T(2,128)(2,1)S(1)}, u32[]{:S(2)}, u32[]{:S(2)}) async-start(bf16[16,2,195]{2,1,0:T(2,128)(2,1)} %reshape.46), calls=%async_computation | async-start | bytes 32768 | tf_op jit(solution)/shard_map/all_to_all | solution.py:56
  230.9 1.7 copy-start.2
  475.9 120.6 %copy-start.1 = (bf16[24,130]{1,0:T(8,128)(2,1)S(1)}, bf16[24,130]{1,0:T(8,128)(2,1)}, u32[]{:S(2)}) copy-start(bf16[24,130]{1,0:T(8,128)(2,1)} %param.8) | copy-start | bytes 18724
  477.6 118.7 %all-to-all-start.2 = ((bf16[16,2,195]{2,1,0:T(2,128)(2,1)}), bf16[16,2,195]{2,1,0:T(2,128)(2,1)S(1)}, u32[]{:S(2)}, u32[]{:S(2)}) async-start(bf16[16,2,195]{2,1,0:T(2,128)(2,1)} %reshape.50), calls=%async_computation.2 | async-start | bytes 32768 | tf_op jit(solution)/shard_map/all_to_all | solution.py:81
where the time goes:
time: 598 us; the launch traced here: 597 us
  blocking collectives  437 us (73%)
  starting transfers between devices  132 us (22%)
  waiting for transfers between devices  11.3 us (2%)
  local copies, waits for them, and re-layouts  6.88 us (1%)
  matrix products  6.08 us (1%)
    unnamed x2, blocking collectives  363 us
    all_to_all x1, starting transfers between devices, local(): lax.all_to_all(mine_grad, 'expert', split_axis=1, concat_axis=0, tiled=True)  111 us
    all_gather x1, blocking collectives, local(): lax.all_gather(x_mine, 'shard', axis=0, tiled=True)  37.5 us
    all_gather x1, blocking collectives, local(): lax.all_gather(g_mine, 'shard', axis=0, tiled=True)  36.3 us
    all_to_all x1, starting transfers between devices, local(): lax.all_to_all(x_send, 'expert', split_axis=0, concat_axis=2, tiled=True)  17.4 us
  transfers between devices with their start and end apart: 3, of which 2 were waited for; matrix products, arithmetic and copies ran while one was open for 1% of the time, Pallas kernels for 0%

commit v1 on v0

v1 whole, which is shorter than its diff:
```python
import functools
import math

import jax
import jax.numpy as jnp
from jax import lax
from jax.experimental import pallas as pl
from jax.experimental.pallas import tpu as pltpu
from jax.sharding import PartitionSpec as P

CAP = 3
ROWS = 8
MESH = pl.DeviceIdType.MESH
f32 = jnp.float32
bf16 = jnp.bfloat16

root_two_over_pi = 0.7978845608028654
cubic_coef = 0.044715


def gelu_parts(pre_act):
    inner = root_two_over_pi * (pre_act + cubic_coef * pre_act * pre_act * pre_act)
    tanh_val = jnp.tanh(inner)
    value = 0.5 * pre_act * (1.0 + tanh_val)
    slope = 0.5 * (1.0 + tanh_val) + 0.5 * pre_act * (
        1.0 - tanh_val * tanh_val
    ) * root_two_over_pi * (1.0 + 3.0 * cubic_coef * pre_act * pre_act)
    return value, slope


def dot(left, right, contract):
    return lax.dot_general(left, right, ((contract[:1], contract[1:]), ((), ())), preferred_element_type=f32)


def remote(src, dst, send_sem, recv_sem, device):
    return pltpu.make_async_remote_copy(
        src_ref=src, dst_ref=dst, send_sem=send_sem, recv_sem=recv_sem, device_id=device, device_id_type=MESH
    )


class Exchange:
    def __init__(self, src_at, dst, sems, n, me, device_of):
        self.src_at, self.dst, self.sems, self.n, self.me, self.device_of = src_at, dst, sems, n, me, device_of

    def copy(self, d):
        other = lax.rem(self.me + d, self.n)
        return remote(
            self.src_at(other), self.dst.at[self.me], self.sems.at[0, d], self.sems.at[1, self.me], self.device_of(other)
        )

    def order(self):
        return sorted(range(1, self.n), key=lambda d: -min(d, self.n - d))

    def start(self):
        for d in self.order():
            self.copy(d).start()

    def wait_recv(self):
        for d in range(1, self.n):
            other = lax.rem(self.me + d, self.n)
            here = self.dst.at[other]
            remote(here, here, self.sems.at[0, d], self.sems.at[1, other], self.device_of(other)).wait_recv()

    def wait_send(self):
        for d in range(1, self.n):
            self.copy(d).wait_send()


class Chain:
    def __init__(self, blocks, sems, n, me, device_of, plus_parts):
        self.blocks, self.sems, self.n, self.me, self.device_of = blocks, sems, n, me, device_of
        self.parts = 3
        self.rows = blocks.shape[1] // self.parts
        self.plus_parts = plus_parts
        self.steps = n // 2
        self.waited = set()
        self.sent = []

    def block(self, index, part):
        return self.blocks.at[lax.rem(index + 2 * self.n, self.n), pl.ds(part * self.rows, self.rows)]

    def travels(self, way, step, part):
        if step < self.steps - 1:
            return True
        return (part in self.plus_parts) == (way == 0)

    def copy(self, way, step, part):
        sign = 1 if way == 0 else -1
        here = self.block(self.me - sign * step, part)
        device = self.device_of(lax.rem(self.me + sign + self.n, self.n))
        return remote(here, here, self.sems.at[0, way, step, part], self.sems.at[1, way, step, part], device)

    def receive(self, way, step, part):
        if (way, step, part) in self.waited or not self.travels(way, step, part):
            return
        self.waited.add((way, step, part))
        sign = 1 if way == 0 else -1
        here = self.block(self.me - sign * (step + 1), part)
        device = self.device_of(lax.rem(self.me + sign + self.n, self.n))
        remote(here, here, self.sems.at[0, way, step, part], self.sems.at[1, way, step, part], device).wait_recv()

    def send(self, way, step, part):
        if step > 0:
            self.receive(way, step - 1, part)
        if self.travels(way, step, part):
            copy = self.copy(way, step, part)
            copy.start()
            self.sent.append(copy)

    def finish(self):
        for step in range(self.steps):
            for part in range(self.parts):
                for way in (0, 1):
                    self.receive(way, step, part)

    def wait_send(self):
        for copy in self.sent:
            copy.wait_send()


def kernel(
    cfg, tok, og, gate, ids, slots, w1_hbm, w2_hbm,
    tok_out, g1_hbm, g2_hbm,
    w1, w2, wa, wb, w1b,
    send_a, recv_a, flat, gat_a, gat_b, rows_a, rows_b, perm,
    send_da, send_db, recv_da, recv_db, send_2a, send_2b, recv_2a, recv_2b,
    send_e, recv_e, grad1, grad2,
    sem_w, sem_g, sem_a, sem_b1, sem_b2, sem_d1, sem_d2, sem_e,
):
    ne, nz, ny, chunk, lanes_a, lanes_b = cfg
    features = ne * chunk
    half = features // 2
    hidden = w1.shape[0]
    e = lax.axis_index("expert")
    s = lax.axis_index("shard")
    z, y = s // ny, lax.rem(s, ny)

    def at_e(i):
        return (i, s)

    def at_z(i):
        return (e, i * ny + y)

    def at_y(i):
        return (e, z * ny + i)

    load1 = pltpu.make_async_copy(w1_hbm, w1, sem_w.at[0])
    load2 = pltpu.make_async_copy(w2_hbm, w2, sem_w.at[1])
    load1.start()
    load2.start()

    barrier = pltpu.get_barrier_semaphore()

    def greet(device):
        pl.semaphore_signal(barrier, inc=1, device_id=device, device_id_type=MESH)

    for d in range(1, ne):
        greet(at_e(lax.rem(e + d, ne)))
    for d in range(1, nz):
        greet(at_z(lax.rem(z + d, nz)))
    for d in range(1, ny):
        greet(at_y(lax.rem(y + d, ny)))
    in_a = e < ny
    last_shard = jnp.where(in_a, z * ny + e, (e - ny) * ny + y)
    for i in range(ne):
        @pl.when(jnp.logical_or(e != i, s != last_shard))
        def _():
            greet((jnp.int32(i), last_shard))
    own_a = e == y
    own_b = e == ny + z
    owned = jnp.where(jnp.logical_or(own_a, own_b), 1, 0)
    pl.semaphore_wait(barrier, (ne - 1) + (nz - 1) + (ny - 1) + nz + ny - owned)

    key = jnp.where(slots[...] >= 0, ids[...] * ROWS + slots[...], -100)
    row = lax.broadcasted_iota(jnp.int32, (ne * ROWS, tok.shape[0]), 0)
    pick_x = jnp.where(row == key, 1.0, 0.0).astype(bf16)
    pick_g = jnp.where(row == key + CAP, 1.0, 0.0).astype(bf16)
    sent = dot(pick_x, tok[...], (1, 0)) + dot(pick_g, og[...], (1, 0))
    send_a[...] = sent.reshape(ne, ROWS, chunk).astype(bf16)
    dispatch = Exchange(lambda i: send_a.at[i], recv_a, sem_a, ne, e, at_e)
    dispatch.start()
    recv_a[e] = send_a[e]

    row8 = lax.broadcasted_iota(jnp.int32, (ROWS, tok.shape[0]), 0) + e * ROWS
    gate_rows = jnp.sum(jnp.where(row8 == key, gate[...].astype(f32), 0.0), axis=1, keepdims=True)
    flat[:, features - features % 128:] = jnp.zeros((ROWS, flat.shape[1] - features + features % 128), f32)
    flat[:, features:features + 1] = gate_rows

    dispatch.wait_recv()
    for i in range(ne):
        flat[:, i * chunk:(i + 1) * chunk] = recv_a[i].astype(f32)
    gat_a[y] = flat[:, :lanes_a].astype(bf16)
    gat_b[z] = flat[:, lanes_a:].astype(bf16)

    first_a = Exchange(lambda i: gat_a.at[y], gat_a, sem_b1.at[0], ny, y, at_y)
    first_b = Exchange(lambda i: gat_b.at[z], gat_b, sem_b1.at[1], nz, z, at_z)
    first_a.start()
    first_b.start()

    load1.wait()
    load2.wait()
    wa[:hidden] = w1[:, :lanes_a]
    wa[hidden:] = w2[:, :lanes_a]
    rest = features - lanes_a
    wb[:, rest - rest % 128:] = jnp.zeros((2 * hidden, lanes_b - rest + rest % 128), bf16)
    wb[:hidden, :rest] = w1[:, lanes_a:]
    wb[hidden:, :rest] = w2[:, lanes_a:]
    w1b[...] = w1[:, half:]

    def dense(n):
        out = lax.broadcasted_iota(jnp.int32, (2 * CAP * n, n * ROWS), 0)
        src = lax.broadcasted_iota(jnp.int32, (2 * CAP * n, n * ROWS), 1)
        return jnp.where(src == lax.rem(out, n) * ROWS + out // n, 1.0, 0.0).astype(bf16)

    def packed(gat, n):
        return dot(dense(n), gat[...].reshape(n * ROWS, gat.shape[2]), (1, 0)).astype(bf16)

    chain_a = Chain(rows_a, sem_b2.at[0], nz, z, at_z, (0, 1))
    chain_b = Chain(rows_b, sem_b2.at[1], ny, y, at_y, (0,))
    first_a.wait_recv()
    rows_a[z] = packed(gat_a, ny)
    for part in range(3):
        for way in (0, 1):
            chain_a.send(way, 0, part)
    first_b.wait_recv()
    rows_b[y] = packed(gat_b, nz)
    for part in range(3):
        for way in (0, 1):
            chain_b.send(way, 0, part)
    for step in range(1, chain_a.steps):
        for part in range(3):
            for way in (0, 1):
                chain_a.send(way, step, part)
                chain_b.send(way, step, part)
    chain_a.finish()
    chain_b.finish()

    all_a = rows_a[...].reshape(nz * 2 * CAP * ny, lanes_a)
    all_b = rows_b[...].reshape(ny * 2 * CAP * nz, lanes_b)
    count = CAP * nz * ny
    lane = lax.broadcasted_iota(jnp.int32, (count, 2 * hidden), 1)

    def both(product, n, m):
        parts = product.reshape(n, 2, CAP * m, 2 * hidden)
        x_part = parts[:, 0].reshape(count, 2 * hidden)
        g_part = parts[:, 1].reshape(count, 2 * hidden)
        return jnp.where(lane < hidden, x_part, g_part)

    def reorder(value, n, m):
        for i in range(value.shape[1] // 128 + (value.shape[1] % 128 > 0)):
            perm[i, :, :min(128, value.shape[1] - 128 * i)] = value[:, 128 * i:128 * (i + 1)]
        pieces = []
        for j in range(m):
            for c in range(CAP):
                pieces.append(jnp.concatenate(
                    [perm[i, pl.ds(c * m + j, n, stride=CAP * m), :] for i in range(perm.shape[0])], axis=1))
        return jnp.concatenate(pieces, axis=0)[:, :value.shape[1]]

    hid_a = both(dot(all_a, wa[...], (1, 1)), nz, ny)
    hid_b = both(dot(all_b, wb[...], (1, 1)), ny, nz)
    hid = hid_b + reorder(hid_a, nz, ny)
    pre_act, back_grad = hid[:, :hidden], hid[:, hidden:]
    gate_lane = features - lanes_a
    gate_tile = gate_lane // 128 * 128
    gates = rows_b[:, :, gate_tile:gate_tile + 128].astype(f32)[:, :CAP * nz].reshape(count, 128)
    gates = gates[:, gate_lane - gate_tile:gate_lane - gate_tile + 1]
    value, slope = gelu_parts(pre_act)
    used_b = jnp.concatenate([gates * back_grad * slope, gates * value], axis=1)
    used_a = reorder(used_b, ny, nz)

    terms_a = dot(used_a[:, :hidden].astype(bf16), w1[:, :half], (1, 0))
    send_da[...] = terms_a.reshape(nz, CAP, ny, half).astype(bf16)
    sum_a = Exchange(lambda i: send_da.at[i], recv_da, sem_d1.at[0], nz, z, at_z)
    sum_a.start()
    recv_da[z] = send_da[z]
    terms_b = dot(used_b[:, :hidden].astype(bf16), w1b[...], (1, 0))
    send_db[...] = terms_b.reshape(ny, CAP, nz, half).astype(bf16)
    sum_b = Exchange(lambda i: send_db.at[i], recv_db, sem_d1.at[1], ny, y, at_y)
    sum_b.start()
    recv_db[y] = send_db[y]

    def spread(used, n, m):
        parts = used.reshape(n, 1, CAP * m, 2 * hidden)
        column = lax.broadcasted_iota(jnp.int32, parts.shape, 3)
        x_part = jnp.where(column < hidden, parts, 0.0)
        g_part = jnp.where(column < hidden, 0.0, parts)
        return jnp.concatenate([x_part, g_part], axis=1).reshape(n * 2 * CAP * m, 2 * hidden).astype(bf16)

    both_a = dot(spread(used_a, nz, ny), all_a, (0, 0))
    grad1[:, :lanes_a] = both_a[:hidden]
    grad2[:, :lanes_a] = both_a[hidden:]
    both_b = dot(spread(used_b, ny, nz), all_b, (0, 0))
    grad1[:, lanes_a:] = both_b[:hidden, :rest]
    grad2[:, lanes_a:] = both_b[hidden:, :rest]
    store1 = pltpu.make_async_copy(grad1, g1_hbm, sem_g.at[0])
    store2 = pltpu.make_async_copy(grad2, g2_hbm, sem_g.at[1])
    store1.start()
    store2.start()

    def second(first, recv, send, again, sems, n, m, me, device_of):
        first.wait_recv()
        total = recv[0].astype(f32)
        for i in range(1, n):
            total = total + recv[i].astype(f32)
        total = total.reshape(CAP * m, half)
        for j in range(m):
            send[j] = total[:, j * chunk:(j + 1) * chunk]
        exchange = Exchange(lambda i: send.at[i], again, sems, m, me, device_of)
        exchange.start()
        again[me] = send[me]
        return exchange

    again_a = second(sum_a, recv_da, send_2a, recv_2a, sem_d2.at[0], nz, ny, y, at_y)
    again_b = second(sum_b, recv_db, send_2b, recv_2b, sem_d2.at[1], ny, nz, z, at_z)

    def by_device(m):
        out = lax.broadcasted_iota(jnp.int32, (m * ROWS, CAP * m), 0)
        src = lax.broadcasted_iota(jnp.int32, (m * ROWS, CAP * m), 1)
        same = src == lax.rem(out, ROWS) * m + out // ROWS
        return jnp.where(jnp.logical_and(lax.rem(out, ROWS) < CAP, same), 1.0, 0.0).astype(bf16)

    def finish(exchange, again, m, send):
        exchange.wait_recv()
        total = again[0]
        for i in range(1, m):
            total = total + again[i]
        picked = dot(by_device(m), total.astype(bf16), (1, 0))
        send[...] = picked.reshape(m, ROWS, chunk).astype(bf16)

    finish(again_a, recv_2a, ny, send_e.at[0, :ny])

    def home(which, index, m, me, expert, shard_of, own):
        other = lax.rem(me + index, m)
        copy = remote(
            send_e.at[which, other], recv_e.at[e], sem_e.at[0, which * ny + index], sem_e.at[1, e],
            (expert, shard_of(other)),
        )
        if index > 0:
            return copy, None
        return copy, own

    homes = []
    for index in range(ny):
        homes.append(home(0, index, ny, y, y, lambda i: z * ny + i, own_a))

    def launch(copy, own, which, me):
        if own is None:
            copy.start()
        else:
            @pl.when(jnp.logical_not(own))
            def _():
                copy.start()

            @pl.when(own)
            def _():
                recv_e[e] = send_e[which, me]

    for copy, own in homes:
        launch(copy, own, 0, y)
    finish(again_b, recv_2b, nz, send_e.at[1, :nz])
    homes_b = []
    for index in range(nz):
        homes_b.append(home(1, index, nz, z, ny + z, lambda i: i * ny + y, own_b))
    for copy, own in homes_b:
        launch(copy, own, 1, z)

    for i in range(ne):
        here = recv_e.at[i]

        @pl.when(jnp.logical_or(e != i, s != last_shard))
        def _():
            remote(here, here, sem_e.at[0, 0], sem_e.at[1, i], (jnp.int32(i), last_shard)).wait_recv()

    branch = dot(pick_x, recv_e[...].reshape(ne * ROWS, chunk), (0, 0))
    tok_out[...] = (og[...].astype(f32) + branch).astype(bf16)

    for exchange in (dispatch, first_a, first_b, chain_a, chain_b, sum_a, sum_b, again_a, again_b):
        exchange.wait_send()
    for copy, own in homes + homes_b:
        if own is None:
            copy.wait_send()
        else:
            @pl.when(jnp.logical_not(own))
            def _():
                copy.wait_send()
    store1.wait()
    store2.wait()


def local(nz, ny, tokens, out_grad, gate_probs, expert_ids, slots, w_in, w_out):
    ne = lax.axis_size("expert")
    count, chunk = tokens.shape
    features = ne * chunk
    half = features // 2
    tiles = (features + 128) // 128
    lanes_a = 128 * ((tiles + 1) // 2)
    lanes_b = 128 * tiles - lanes_a
    w1 = jnp.swapaxes(w_in[0], 0, 1)
    w2 = w_out[0]
    hidden = w1.shape[0]
    cfg = (ne, nz, ny, chunk, lanes_a, lanes_b)
    vmem = pltpu.VMEM
    dma = pltpu.SemaphoreType.DMA
    most = max(nz, ny)
    scratch = [
        vmem((hidden, features), bf16),
        vmem((hidden, features), bf16),
        vmem((2 * hidden, lanes_a), bf16),
        vmem((2 * hidden, lanes_b), bf16),
        vmem((hidden, half), bf16),
        vmem((ne, ROWS, chunk), bf16),
        vmem((ne, ROWS, chunk), bf16),
        vmem((ROWS, lanes_a + lanes_b), f32),
        vmem((ny, ROWS, lanes_a), bf16),
        vmem((nz, ROWS, lanes_b), bf16),
        vmem((nz, 2 * CAP * ny, lanes_a), bf16),
        vmem((ny, 2 * CAP * nz, lanes_b), bf16),
        vmem((math.ceil(2 * hidden / 128), CAP * nz * ny, 128), f32),
        vmem((nz, CAP, ny, half), bf16),
        vmem((ny, CAP, nz, half), bf16),
        vmem((nz, CAP, ny, half), bf16),
        vmem((ny, CAP, nz, half), bf16),
        vmem((ny, CAP * ny, chunk), f32),
        vmem((nz, CAP * nz, chunk), f32),
        vmem((ny, CAP * ny, chunk), f32),
        vmem((nz, CAP * nz, chunk), f32),
        vmem((2, most, ROWS, chunk), bf16),
        vmem((ne, ROWS, chunk), bf16),
        vmem((hidden, features), f32),
        vmem((hidden, features), f32),
        dma((2,)),
        dma((2,)),
        dma((2, ne)),
        dma((2, 2, most)),
        dma((2, 2, 2, most // 2, 3)),
        dma((2, 2, most)),
        dma((2, 2, most)),
        dma((2, ne)),
    ]
    in_vmem = pl.BlockSpec(memory_space=pltpu.VMEM)
    anywhere = pl.BlockSpec(memory_space=pl.ANY)
    token_grad, g1, g2 = pl.pallas_call(
        functools.partial(kernel, cfg),
        out_shape=(
            jax.ShapeDtypeStruct((count, chunk), bf16),
            jax.ShapeDtypeStruct((hidden, features), f32),
            jax.ShapeDtypeStruct((hidden, features), f32),
        ),
        in_specs=[in_vmem] * 5 + [anywhere] * 2,
        out_specs=(in_vmem, anywhere, anywhere),
        scratch_shapes=scratch,
        compiler_params=pltpu.CompilerParams(
            collective_id=0, has_side_effects=True, vmem_limit_bytes=48 * 1024 * 1024
        ),
        name="moe_backward",
    )(tokens, out_grad, gate_probs[None], expert_ids[None], slots[None], w1, w2)
    return token_grad, jnp.swapaxes(g1, 0, 1)[None], g2[None]


def solution(mesh):
    placed = (
        P("shard", "expert"),
        P("shard", "expert"),
        P("shard"),
        P("shard"),
        P("shard"),
        P("expert", None, "shard"),
        P("expert", "shard", None),
    )
    ny = math.isqrt(mesh.shape["shard"])
    nz = mesh.shape["shard"] // ny
    return jax.shard_map(
        functools.partial(local, nz, ny),
        mesh=mesh,
        in_specs=placed,
        out_specs=(P("shard", "expert"), P("expert", None, "shard"), P("expert", "shard", None)),
        check_vma=False,
    )
```

time: 598 us -> 86 us (0.14)
  blocking collectives: 437 us -> 0 us
  starting transfers between devices: 132 us -> 0 us
  Pallas kernels: 0 us -> 77.3 us
  waiting for transfers between devices: 11.3 us -> 0 us
  matrix products: 6.08 us -> 0 us
    unnamed x2 -> x0, blocking collectives: 363 us -> none
    all_to_all x3 -> x0, starting transfers between devices: 132 us -> none  [the longest x1 111 us: local(): lax.all_to_all(mine_grad, 'expert', split_axis=1, concat_axis=0, tiled=True)]
    pallas_call x0 -> x1, Pallas kernels: none -> 77.3 us  [local(): pl.pallas_call(functools.partial(kernel, cfg), out_shape=(jax.ShapeDtypeS...]
    all_gather x2 -> x0, blocking collectives: 73.8 us -> none  [the longest x1 37.5 us: local(): lax.all_gather(x_mine, 'shard', axis=0, tiled=True)]
    all_to_all x3 -> x0, waiting for transfers between devices: 11.3 us -> none  [the longest x1 6.11 us: local(): lax.all_to_all(mine_grad, 'expert', split_axis=1, concat_axis=0, tiled=True)]
    dot_general x8 -> x0, matrix products: 6.08 us -> none  [the longest x3 3.29 us: inner_rows(): lax.dot_general(left, right, (((0,), (0,)), ((), ())), preferred_element_...]
  transfers between devices with their start and end apart: 3 -> 0, of which waited for: 2 -> 0; matrix products, arithmetic and copies ran while one was open for 1% -> 0% of each run, Pallas kernels for 0% -> 0%
where the time goes in v1:
time: 86 us; the launch traced here: 84.4 us
  Pallas kernels  77.3 us (90%)
  local copies, waits for them, and re-layouts  6.48 us (8%)
    pallas_call x1, Pallas kernels, local(): pl.pallas_call(functools.partial(kernel, cfg), out_shape=(jax.ShapeDtypeS...  77.3 us
    unnamed x17, local copies, waits for them, and re-layouts  6.48 us

profile of v1, /device:TPU:1, one launch (start us, length us, event | category | flops | bytes accessed | tf_op | source)
XLA Modules:
  0.0 84.4 jit_solution(15119703565074443150)
XLA Ops:
  0.6 0.0 copy-start.4
  0.6 0.0 copy-start.5
  0.7 0.0 copy-start.6
  0.7 0.6 copy-done.4
  1.3 0.0 copy-done.5
  1.3 0.0 copy-done.6
  1.3 0.0 copy-start
  1.3 1.0 %copy-done = bf16[1,2080,96]{1,2,0:T(8,128)(2,1)S(1)} copy-done((bf16[1,2080,96]{1,2,0:T(8,128)(2,1)S(1)}, bf16[1,2080,96]{1,2,0:T(8,128)(2,1)}, u32[]{:S(2)}) %copy-start) | copy-done | bytes 399384
  2.3 0.0 copy-start.1
  2.3 1.0 %copy-done.1 = bf16[1,96,2080]{2,1,0:T(8,128)(2,1)S(1)} copy-done((bf16[1,96,2080]{2,1,0:T(8,128)(2,1)S(1)}, bf16[1,96,2080]{2,1,0:T(8,128)(2,1)}, u32[]{:S(2)}) %copy-start.1) | copy-done | bytes 399384
  3.3 0.0 copy-start.2
  3.3 0.7 copy-done.2
  4.0 0.0 copy-start.3
  4.0 0.7 copy-done.3
  4.7 77.3 %moe_backward.1 = (bf16[24,130]{1,0:T(8,128)(2,1)S(1)}, f32[96,2080]{1,0:T(8,128)S(1)}, f32[96,2080]{1,0:T(8,128)S(1)}) custom-call(bf16[24,130]{1,0:T(8,128)(2,1)S(1)} %copy-done.2, bf16[24,130]{1,0:T(8,128)(2,1)S(1)} %copy-done.3, bf16[1,24]{1,0:T(2,128)(2,1)S(1)} %bitcast.15, s32[1,24]{1,0:T(1,128)S(1)} %bitcast.16, s32[1,24]{1,0:T(1,128)S(1)} %bitcast.17, ...), custom_call_target="tpu_custom_call" | custom-call | tf_op jit(solution)/shard_map/moe_backward/pallas_call | solution.py:442
  82.1 0.6 copy.13
  82.7 0.9 %copy.14 = f32[1,2080,96]{1,2,0:T(8,128)} copy(f32[1,2080,96]{1,2,0:T(8,128)S(1)} %bitcast.12) | data formatting | bytes 1597440
  83.6 0.9 %copy.15 = f32[1,96,2080]{2,1,0:T(8,128)} copy(f32[1,96,2080]{2,1,0:T(8,128)S(1)} %bitcast.11) | data formatting | bytes 1597440
Async XLA Ops:
  0.6 0.7 copy-start.4
  0.6 0.7 copy-start.5
  0.7 0.7 copy-start.6
  1.3 1.0 %copy-start = (bf16[1,2080,96]{1,2,0:T(8,128)(2,1)S(1)}, bf16[1,2080,96]{1,2,0:T(8,128)(2,1)}, u32[]{:S(2)}) copy-start(bf16[1,2080,96]{1,2,0:T(8,128)(2,1)} %param.12) | copy-start | bytes 1198084
  2.3 1.0 %copy-start.1 = (bf16[1,96,2080]{2,1,0:T(8,128)(2,1)S(1)}, bf16[1,96,2080]{2,1,0:T(8,128)(2,1)}, u32[]{:S(2)}) copy-start(bf16[1,96,2080]{2,1,0:T(8,128)(2,1)} %param.13) | copy-start | bytes 1198084
  3.3 0.7 copy-start.2
  4.0 0.7 copy-start.3

commit v2 on v0

v2 whole, which is shorter than its diff:
```python
import functools
import math

import jax
import jax.numpy as jnp
from jax import lax
from jax.experimental import pallas as pl
from jax.experimental.pallas import tpu as pltpu
from jax.sharding import PartitionSpec as P

CAP = 3
ROWS = 8
MESH = pl.DeviceIdType.MESH
f32 = jnp.float32
bf16 = jnp.bfloat16

root_two_over_pi = 0.7978845608028654
cubic_coef = 0.044715


def gelu_parts(pre_act):
    inner = root_two_over_pi * (pre_act + cubic_coef * pre_act * pre_act * pre_act)
    tanh_val = jnp.tanh(inner)
    value = 0.5 * pre_act * (1.0 + tanh_val)
    slope = 0.5 * (1.0 + tanh_val) + 0.5 * pre_act * (
        1.0 - tanh_val * tanh_val
    ) * root_two_over_pi * (1.0 + 3.0 * cubic_coef * pre_act * pre_act)
    return value, slope


def dot(left, right, contract):
    return lax.dot_general(left, right, ((contract[:1], contract[1:]), ((), ())), preferred_element_type=f32)


def remote(src, dst, send_sem, recv_sem, device):
    return pltpu.make_async_remote_copy(
        src_ref=src, dst_ref=dst, send_sem=send_sem, recv_sem=recv_sem, device_id=device, device_id_type=MESH
    )


class Exchange:
    def __init__(self, src, dst, got, sems, n, me, device_of):
        self.src, self.dst, self.got, self.sems, self.n, self.me, self.device_of = src, dst, got, sems, n, me, device_of

    def copy(self, d):
        device = self.device_of(lax.rem(self.me + d, self.n))
        return remote(self.src(d), self.dst(d), self.sems.at[0, d], self.sems.at[1, d], device)

    def start(self, order):
        for d in order:
            self.copy(d).start()

    def wait_recv(self, order):
        for d in order:
            here = self.got(d)
            device = self.device_of(lax.rem(self.me + self.n - d, self.n))
            remote(here, here, self.sems.at[0, d], self.sems.at[1, d], device).wait_recv()

    def wait_send(self):
        for d in range(1, self.n):
            self.copy(d).wait_send()


def far_first(n):
    return sorted(range(1, n), key=lambda d: -min(d, n - d))


class Spread:
    def __init__(self, blocks, sems, n, me, device_of):
        self.blocks, self.sems, self.n, self.me, self.device_of = blocks, sems, n, me, device_of
        self.waited = set()
        self.sent = []
        if n > 4:
            self.first = {0: (-2, 2), 1: (2, -2), 2: (-1, 1), 3: (1, -1)}
            self.second = {4: (-3, 1), 5: (3, -1), 6: (4, 2), 7: (4, -2)}
        else:
            self.first = {0: (1, 1)}
            self.second = {}

    def block(self, distance, part):
        return self.blocks.at[(distance + self.n // 2 - 1) % self.n, part]

    def copy(self, index, part):
        distance, places = {**self.first, **self.second}[index]
        device = self.device_of(lax.rem(self.me + places + self.n, self.n))
        src, dst = self.block(distance + places, part), self.block(distance, part)
        return remote(src, dst, self.sems.at[0, index, part], self.sems.at[1, index, part], device)

    def send(self, index, part):
        copy = self.copy(index, part)
        copy.start()
        self.sent.append(copy)

    def receive(self, index, part):
        if (index, part) in self.waited:
            return
        self.waited.add((index, part))
        distance, places = {**self.first, **self.second}[index]
        device = self.device_of(lax.rem(self.me - places + self.n, self.n))
        here = self.block(distance, part)
        remote(here, here, self.sems.at[0, index, part], self.sems.at[1, index, part], device).wait_recv()

    def start(self, part):
        for index in self.first:
            self.send(index, part)

    def forward(self, part):
        if self.second:
            for index, through, across in ((0, 4, 6), (1, 5, 7)):
                self.receive(index, part)
                if part == index:
                    self.send(across, part)
                self.send(through, part)

    def finish(self, part):
        for index in self.first:
            self.receive(index, part)
        if self.second:
            for index in (4, 5, 6 + part):
                self.receive(index, part)

    def wait_send(self):
        for copy in self.sent:
            copy.wait_send()


def kernel(
    cfg, tok_hbm, og_hbm, gate_hbm, ids_hbm, slots_hbm, w1_hbm, w2_hbm,
    tok_out, grad1, grad2,
    tok, og, gate, ids, slots, w1, w2, wa, wb, w1b,
    send_a, recv_a, flat, gat_a, gat_b, rows_a, rows_b, hid_a, hid_b, used, used_a, used_b,
    send_da, send_db, recv_da, recv_db, fold, send_2a, send_2b, recv_2a, recv_2b,
    send_e, recv_e,
    sem_w, sem_a, sem_b1, sem_b2, sem_d1, sem_d2, sem_e,
):
    ne, nz, ny, chunk, lanes_a, lanes_b = cfg
    n = nz
    features = ne * chunk
    half = features // 2
    rest = features - lanes_a
    hidden = w1.shape[0]
    per = 2 * CAP
    block_rows = n * per
    count = CAP * n * n
    e = lax.axis_index("expert")
    s = lax.axis_index("shard")
    z, y = s // ny, lax.rem(s, ny)

    def at_e(i):
        return (i, s)

    def at_z(i):
        return (e, i * ny + y)

    def at_y(i):
        return (e, z * ny + i)

    barrier = pltpu.get_barrier_semaphore()
    for device_of, me, size in ((at_e, e, ne), (at_z, z, nz), (at_y, y, ny)):
        for d in far_first(size):
            pl.semaphore_signal(barrier, inc=1, device_id=device_of(lax.rem(me + d, size)), device_id_type=MESH)

    sources = (tok_hbm, og_hbm, gate_hbm, ids_hbm, slots_hbm, w1_hbm, w2_hbm)
    places = (tok, og, gate, ids, slots, w1, w2)
    loads = [pltpu.make_async_copy(src, dst, sem_w.at[i]) for i, (src, dst) in enumerate(zip(sources, places))]
    for load in loads:
        load.start()

    for load in loads[:5]:
        load.wait()
    key = jnp.where(slots[...] >= 0, ids[...] * ROWS + slots[...], -100)
    row = lax.broadcasted_iota(jnp.int32, (ne * ROWS, tok.shape[0]), 0)
    pick_x = jnp.where(row == key, 1.0, 0.0).astype(bf16)
    pick_g = jnp.where(row == key + CAP, 1.0, 0.0).astype(bf16)
    sent = dot(pick_x, tok[...], (1, 0)) + dot(pick_g, og[...], (1, 0))
    send_a[...] = sent.reshape(ne, ROWS, chunk).astype(bf16)
    row8 = lax.broadcasted_iota(jnp.int32, (ROWS, tok.shape[0]), 0) + e * ROWS
    gate_rows = jnp.sum(jnp.where(row8 == key, gate[...].astype(f32), 0.0), axis=1, keepdims=True)
    flat[:, features - features % 128:] = jnp.zeros((ROWS, flat.shape[1] - features + features % 128), f32)
    flat[:, features:features + 1] = gate_rows

    pl.semaphore_wait(barrier, (ne - 1) + (nz - 1) + (ny - 1))

    dispatch = Exchange(
        lambda d: send_a.at[lax.rem(e + d, ne)], lambda d: recv_a.at[e], lambda d: recv_a.at[lax.rem(e + ne - d, ne)],
        sem_a, ne, e, at_e)
    dispatch.start(far_first(ne))
    recv_a[e] = send_a[e]

    loads[5].wait()
    loads[6].wait()
    wa[...] = jnp.zeros(wa.shape, bf16)
    wb[...] = jnp.zeros(wb.shape, bf16)
    wa[:hidden] = w1[:, :lanes_a]
    wa[128:128 + hidden] = w2[:, :lanes_a]
    wb[:hidden, :rest] = w1[:, lanes_a:]
    wb[128:128 + hidden, :rest] = w2[:, lanes_a:]
    gate_unit = lax.broadcasted_iota(jnp.int32, (16, lanes_b), 0) == 0
    gate_lane = lax.broadcasted_iota(jnp.int32, (16, lanes_b), 1) == rest
    wb[hidden:hidden + 16] = jnp.where(jnp.logical_and(gate_unit, gate_lane), 1.0, 0.0).astype(bf16)
    w1b[...] = w1[:, half:]
    used_a[...] = jnp.zeros(used_a.shape, f32)
    used_b[...] = jnp.zeros(used_b.shape, f32)
    send_2a[...] = jnp.zeros(send_2a.shape, f32)
    send_2b[...] = jnp.zeros(send_2b.shape, f32)

    dispatch.wait_recv(range(1, ne))
    for i in range(ne):
        flat[:, i * chunk:(i + 1) * chunk] = recv_a[i].astype(f32)

    def place(distance):
        return (distance + 1) % n

    def first(gat, sems, me, device_of):
        mine = place(0)
        return Exchange(lambda d: gat.at[mine], lambda d: gat.at[place(-d)], lambda d: gat.at[place(-d)], sems, n, me, device_of)

    near = [d for d in range(1, n) if place(-d) < n // 2]
    far = [d for d in range(1, n) if place(-d) >= n // 2]
    first_a = first(gat_a, sem_b1.at[0], y, at_y)
    first_b = first(gat_b, sem_b1.at[1], z, at_z)
    gat_a[place(0)] = flat[:, :lanes_a].astype(bf16)
    first_a.start(near + far)
    gat_b[place(0)] = flat[:, lanes_a:].astype(bf16)
    first_b.start(near + far)

    out = lax.broadcasted_iota(jnp.int32, (block_rows // 2, n // 2 * ROWS), 0)
    src = lax.broadcasted_iota(jnp.int32, (block_rows // 2, n // 2 * ROWS), 1)
    dense = jnp.where(src == out // per * ROWS + lax.rem(out, per), 1.0, 0.0).astype(bf16)

    def packed(gat, part):
        piece = gat[part * (n // 2):(part + 1) * (n // 2)]
        return dot(dense, piece.reshape(n // 2 * ROWS, gat.shape[2]), (1, 0))

    spread_a = Spread(rows_a, sem_b2.at[0], nz, z, at_z)
    spread_b = Spread(rows_b, sem_b2.at[1], ny, y, at_y)
    for part, group in ((0, near), (1, far)):
        for exchange, spread, gat in ((first_a, spread_a, gat_a), (first_b, spread_b, gat_b)):
            exchange.wait_recv(group)
            blocks = spread.blocks
            blocks[n // 2 - 1, part] = packed(gat, part).reshape(blocks.shape[2:]).astype(bf16)
            spread.start(part)
    for part in (0, 1):
        for spread in (spread_a, spread_b):
            spread.forward(part)
    for part in (0, 1):
        for spread in (spread_a, spread_b):
            spread.finish(part)

    def block_of(i):
        return (i - 1 + n // 2 - 1) % n

    all_a = rows_a[...].reshape(n * block_rows, lanes_a)
    all_b = rows_b[...].reshape(n * block_rows, lanes_b)
    for hid, rows, weights in ((hid_a, all_a, wa), (hid_b, all_b, wb)):
        product = dot(rows, weights[...], (1, 1))
        for i in range(n):
            here = product[block_of(i) * block_rows:(block_of(i) + 1) * block_rows]
            hid[0, i * block_rows:(i + 1) * block_rows] = here[:, :128]
            hid[1, i * block_rows:(i + 1) * block_rows] = here[:, 128:]

    def gathered(which, q):
        return jnp.concatenate([
            hid_a[which, pl.ds(i * block_rows + q, n, stride=per), :]
            + hid_b[which, pl.ds(i * per + q, n, stride=block_rows), :] for i in range(n)], axis=0)

    for c in range(CAP):
        pre_act = gathered(0, c)
        back_grad = gathered(1, CAP + c)
        gates = pre_act[:, hidden:hidden + 1]
        value, slope = gelu_parts(pre_act)
        used[0, c * n * n:(c + 1) * n * n] = gates * back_grad * slope
        used[1, c * n * n:(c + 1) * n * n] = gates * value

    def terms(rows, weights, send):
        result = dot(rows[:, :hidden].astype(bf16), weights, (1, 0))
        send[...] = result.reshape(send.shape).astype(bf16)

    def first_sum(send, recv, sems, me, device_of):
        return Exchange(lambda d: send.at[place(d)], lambda d: recv.at[d], lambda d: recv.at[d], sems, n, me, device_of)

    order_a = [used[0, (c * n + i) * n:(c * n + i + 1) * n, :] for i in range(n) for c in range(CAP)]
    terms(jnp.concatenate(order_a, axis=0), w1[:, :half], send_da)
    sum_a = first_sum(send_da, recv_da, sem_d1.at[0], z, at_z)
    sum_a.start(far_first(n))
    order_b = [used[0, pl.ds(c * n * n + i, n, stride=n), :] for i in range(n) for c in range(CAP)]
    terms(jnp.concatenate(order_b, axis=0), w1b[...], send_db)
    sum_b = first_sum(send_db, recv_db, sem_d1.at[1], y, at_y)
    sum_b.start(far_first(n))

    for c in range(CAP):
        for i in range(n):
            for which in (0, 1):
                q = which * CAP + c
                piece = used[which, (c * n + i) * n:(c * n + i + 1) * n, :]
                used_a[which, pl.ds(block_of(i) * block_rows + q, n, stride=per), :] = piece
    for c in range(CAP):
        for i in range(n):
            for which in (0, 1):
                q = which * CAP + c
                piece = used[which, pl.ds(c * n * n + i, n, stride=n), :]
                used_b[which, pl.ds(block_of(i) * block_rows + q, n, stride=per), :] = piece

    for pieces, rows, first_lane, width in ((used_a, all_a, 0, lanes_a), (used_b, all_b, lanes_a, rest)):
        both = jnp.concatenate([pieces[0], pieces[1]], axis=1).astype(bf16)
        product = dot(both, rows, (0, 0))
        grad1[:, first_lane:first_lane + width] = product[:hidden, :width]
        grad2[:, first_lane:first_lane + width] = product[128:128 + hidden, :width]

    quarter = half // 2
    tiles = fold.shape[0]

    def second(exchange, send_first, recv, send, again, sems, me, device_of):
        exchange.wait_recv(far_first(n)[::-1])
        total = send_first[place(0)].astype(f32)
        for d in range(1, n):
            total = total + recv[d].astype(f32)
        total = total.reshape(CAP * n, half)
        for h in (0, 1):
            piece = total[:, h * quarter:(h + 1) * quarter]
            for t in range(tiles):
                width = min(128, quarter - 128 * t)
                fold[t, h * CAP * n:(h + 1) * CAP * n, :width] = piece[:, 128 * t:128 * t + width]
        for i in range(n):
            for t in range(tiles):
                width = min(128, quarter - 128 * t)
                send[i, :per, 128 * t:128 * t + width] = fold[t, pl.ds(i, per, stride=n), :][:, :width]
        again_sum = Exchange(lambda d: send.at[place(d)], lambda d: again.at[d], lambda d: again.at[d], sems, n, me, device_of)
        again_sum.start(far_first(n))
        return again_sum

    again_a = second(sum_a, send_da, recv_da, send_2a, recv_2a, sem_d2.at[0], y, at_y)
    again_b = second(sum_b, send_db, recv_db, send_2b, recv_2b, sem_d2.at[1], z, at_z)

    quarter_chunks = ne // 4
    for which, exchange, send, again in ((0, again_a, send_2a, recv_2a), (1, again_b, send_2b, recv_2b)):
        exchange.wait_recv(far_first(n)[::-1])
        total = send[place(0)]
        for d in range(1, n):
            total = total + again[d]
        for i in range(quarter_chunks):
            send_e[which * quarter_chunks + i] = total[:, i * chunk:(i + 1) * chunk].astype(bf16)

    def block_for(i):
        return i // (ne // 2) * quarter_chunks + lax.rem(i, quarter_chunks)

    back = Exchange(
        lambda d: send_e.at[block_for(lax.rem(e + d, ne))], lambda d: recv_e.at[e], lambda d: recv_e.at[lax.rem(e + ne - d, ne)],
        sem_e, ne, e, at_e)
    back.start(far_first(ne))
    recv_e[e] = send_e[block_for(e)]
    my_quarter = lax.rem(e, ne // 2) // quarter_chunks
    pick_e = jnp.where(row == key + my_quarter * CAP, 1.0, 0.0).astype(bf16)
    for exchange in (dispatch, first_a, first_b, spread_a, spread_b, sum_a, sum_b, again_a, again_b):
        exchange.wait_send()
    back.wait_recv(range(1, ne))
    branch = dot(pick_e, recv_e[...].reshape(ne * ROWS, chunk), (0, 0))
    tok_out[...] = (og[...].astype(f32) + branch).astype(bf16)
    back.wait_send()


def local(nz, ny, tokens, out_grad, gate_probs, expert_ids, slots, w_in, w_out):
    ne = lax.axis_size("expert")
    n = nz
    tokens_here, chunk = tokens.shape
    features = ne * chunk
    half = features // 2
    tiles = (features + 128) // 128
    lanes_a = 128 * ((tiles + 1) // 2)
    lanes_b = 128 * tiles - lanes_a
    w1 = jnp.swapaxes(w_in[0], 0, 1)
    w2 = w_out[0]
    hidden = w1.shape[0]
    cfg = (ne, nz, ny, chunk, lanes_a, lanes_b)
    vmem = pltpu.VMEM
    dma = pltpu.SemaphoreType.DMA
    per = 2 * CAP
    part_rows = n * per // 2
    step_rows = math.gcd(8, part_rows)
    scratch = [
        vmem((tokens_here, chunk), bf16),
        vmem((tokens_here, chunk), bf16),
        vmem((1, tokens_here), bf16),
        vmem((1, tokens_here), jnp.int32),
        vmem((1, tokens_here), jnp.int32),
        vmem((hidden, features), bf16),
        vmem((hidden, features), bf16),
        vmem((256, lanes_a), bf16),
        vmem((256, lanes_b), bf16),
        vmem((hidden, half), bf16),
        vmem((ne, ROWS, chunk), bf16),
        vmem((ne, ROWS, chunk), bf16),
        vmem((ROWS, lanes_a + lanes_b), f32),
        vmem((n, ROWS, lanes_a), bf16),
        vmem((n, ROWS, lanes_b), bf16),
        vmem((n, 2, part_rows // step_rows, step_rows, lanes_a), bf16),
        vmem((n, 2, part_rows // step_rows, step_rows, lanes_b), bf16),
        vmem((2, n * n * per, 128), f32),
        vmem((2, n * n * per, 128), f32),
        vmem((2, CAP * n * n, 128), f32),
        vmem((2, n * n * per, 128), f32),
        vmem((2, n * n * per, 128), f32),
        vmem((n, CAP, n, half), bf16),
        vmem((n, CAP, n, half), bf16),
        vmem((n, CAP, n, half), bf16),
        vmem((n, CAP, n, half), bf16),
        vmem((math.ceil(half // 2 / 128), per * n, 128), f32),
        vmem((n, ROWS, half // 2), f32),
        vmem((n, ROWS, half // 2), f32),
        vmem((n, ROWS, half // 2), f32),
        vmem((n, ROWS, half // 2), f32),
        vmem((ne // 2, ROWS, chunk), bf16),
        vmem((ne, ROWS, chunk), bf16),
        dma((7,)),
        dma((2, ne)),
        dma((2, 2, n)),
        dma((2, 2, 8, 2)),
        dma((2, 2, n)),
        dma((2, 2, n)),
        dma((2, ne)),
    ]
    in_vmem = pl.BlockSpec(memory_space=pltpu.VMEM)
    in_hbm = pl.BlockSpec(memory_space=pltpu.HBM)
    operands = (tokens, out_grad, gate_probs[None], expert_ids[None], slots[None], w1, w2)
    token_grad, g1, g2 = pl.pallas_call(
        functools.partial(kernel, cfg),
        out_shape=(
            jax.ShapeDtypeStruct((tokens_here, chunk), bf16),
            jax.ShapeDtypeStruct((hidden, features), f32),
            jax.ShapeDtypeStruct((hidden, features), f32),
        ),
        in_specs=[in_hbm] * 7,
        out_specs=(in_vmem,) * 3,
        scratch_shapes=scratch,
        compiler_params=pltpu.CompilerParams(
            collective_id=0, has_side_effects=True, vmem_limit_bytes=48 * 1024 * 1024
        ),
        name="moe_backward",
    )(*[pltpu.with_memory_space_constraint(value, pltpu.HBM) for value in operands])
    return token_grad, jnp.swapaxes(g1, 0, 1)[None], g2[None]


def solution(mesh):
    placed = (
        P("shard", "expert"),
        P("shard", "expert"),
        P("shard"),
        P("shard"),
        P("shard"),
        P("expert", None, "shard"),
        P("expert", "shard", None),
    )
    ny = math.isqrt(mesh.shape["shard"])
    nz = mesh.shape["shard"] // ny
    return jax.shard_map(
        functools.partial(local, nz, ny),
        mesh=mesh,
        in_specs=placed,
        out_specs=(P("shard", "expert"), P("expert", None, "shard"), P("expert", "shard", None)),
        check_vma=False,
    )
```

time: 598 us -> 73.5 us (0.12)
  blocking collectives: 437 us -> 0 us
  starting transfers between devices: 132 us -> 0 us
  Pallas kernels: 0 us -> 70.3 us
  waiting for transfers between devices: 11.3 us -> 0 us
  matrix products: 6.08 us -> 0 us
    unnamed x2 -> x0, blocking collectives: 363 us -> none
    all_to_all x3 -> x0, starting transfers between devices: 132 us -> none  [the longest x1 111 us: local(): lax.all_to_all(mine_grad, 'expert', split_axis=1, concat_axis=0, tiled=True)]
    all_gather x2 -> x0, blocking collectives: 73.8 us -> none  [the longest x1 37.5 us: local(): lax.all_gather(x_mine, 'shard', axis=0, tiled=True)]
    pallas_call x0 -> x1, Pallas kernels: none -> 70.3 us  [local(): pl.pallas_call(functools.partial(kernel, cfg), out_shape=(jax.ShapeDtypeS...]
    all_to_all x3 -> x0, waiting for transfers between devices: 11.3 us -> none  [the longest x1 6.11 us: local(): lax.all_to_all(mine_grad, 'expert', split_axis=1, concat_axis=0, tiled=True)]
    dot_general x8 -> x0, matrix products: 6.08 us -> none  [the longest x3 3.29 us: inner_rows(): lax.dot_general(left, right, (((0,), (0,)), ((), ())), preferred_element_...]
  transfers between devices with their start and end apart: 3 -> 0, of which waited for: 2 -> 0; matrix products, arithmetic and copies ran while one was open for 1% -> 0% of each run, Pallas kernels for 0% -> 0%
where the time goes in v2:
time: 73.5 us; the launch traced here: 73.3 us
  Pallas kernels  70.3 us (96%)
  local copies, waits for them, and re-layouts  2.39 us (3%)
    pallas_call x1, Pallas kernels, local(): pl.pallas_call(functools.partial(kernel, cfg), out_shape=(jax.ShapeDtypeS...  70.3 us
    unnamed x3, local copies, waits for them, and re-layouts  2.39 us

profile of v2, /device:TPU:1, one launch (start us, length us, event | category | flops | bytes accessed | tf_op | source)
XLA Modules:
  0.0 73.3 jit_solution(14182591515077030345)
XLA Ops:
  0.6 70.3 %moe_backward.1 = (bf16[24,130]{1,0:T(8,128)(2,1)S(1)}, f32[96,2080]{1,0:T(8,128)S(1)}, f32[96,2080]{1,0:T(8,128)S(1)}) custom-call(bf16[24,130]{1,0:T(8,128)(2,1)} %tok_hbm.1, bf16[24,130]{1,0:T(8,128)(2,1)} %og_hbm.1, bf16[1,24]{1,0:T(2,128)(2,1)} %bitcast.15, s32[1,24]{1,0:T(1,128)} %bitcast.16, s32[1,24]{1,0:T(1,128)} %bitcast.17, ...), custom_call_target="tpu_custom_call" | custom-call | tf_op jit(solution)/shard_map/moe_backward/pallas_call | solution.py:425
  71.0 0.6 copy.13
  71.6 0.9 %copy.14 = f32[1,2080,96]{1,2,0:T(8,128)} copy(f32[1,2080,96]{1,2,0:T(8,128)S(1)} %bitcast.12) | data formatting | bytes 1597440
  72.4 0.9 %copy.15 = f32[1,96,2080]{2,1,0:T(8,128)} copy(f32[1,96,2080]{2,1,0:T(8,128)S(1)} %bitcast.11) | data formatting | bytes 1597440

commit v3 on v2

--- a/solution.py
+++ b/solution.py
@@ -129,7 +129,7 @@
     tok_out, grad1, grad2,
     tok, og, gate, ids, slots, w1, w2, wa, wb, w1b,
     send_a, recv_a, flat, gat_a, gat_b, rows_a, rows_b, hid_a, hid_b, used, used_a, used_b,
-    send_da, send_db, recv_da, recv_db, fold, send_2a, send_2b, recv_2a, recv_2b,
+    send_da, send_db, recv_da, recv_db, send_2a, send_2b, recv_2a, recv_2b,
     send_e, recv_e,
     sem_w, sem_a, sem_b1, sem_b2, sem_d1, sem_d2, sem_e,
 ):
@@ -155,16 +155,16 @@
     def at_y(i):
         return (e, z * ny + i)
 
-    barrier = pltpu.get_barrier_semaphore()
-    for device_of, me, size in ((at_e, e, ne), (at_z, z, nz), (at_y, y, ny)):
-        for d in far_first(size):
-            pl.semaphore_signal(barrier, inc=1, device_id=device_of(lax.rem(me + d, size)), device_id_type=MESH)
-
     sources = (tok_hbm, og_hbm, gate_hbm, ids_hbm, slots_hbm, w1_hbm, w2_hbm)
     places = (tok, og, gate, ids, slots, w1, w2)
     loads = [pltpu.make_async_copy(src, dst, sem_w.at[i]) for i, (src, dst) in enumerate(zip(sources, places))]
     for load in loads:
         load.start()
+
+    barrier = pltpu.get_barrier_semaphore()
+    for device_of, me, size in ((at_e, e, ne), (at_z, z, nz), (at_y, y, ny)):
+        for d in far_first(size):
+            pl.semaphore_signal(barrier, inc=1, device_id=device_of(lax.rem(me + d, size)), device_id_type=MESH)
 
     for load in loads[:5]:
         load.wait()
@@ -207,6 +207,11 @@
     dispatch.wait_recv(range(1, ne))
     for i in range(ne):
         flat[:, i * chunk:(i + 1) * chunk] = recv_a[i].astype(f32)
+    for base, gat in ((0, gat_a), (lanes_a, gat_b)):
+        for k in range(ROWS - per):
+            tail = base + gat.shape[2] + 128 * k
+            for q in range(per):
+                flat[per + k:per + k + 1, base + 128 * q:base + 128 * (q + 1)] = flat[q:q + 1, tail:tail + 128]
 
     def place(distance):
         return (distance + 1) % n
@@ -219,18 +224,26 @@
     far = [d for d in range(1, n) if place(-d) >= n // 2]
     first_a = first(gat_a, sem_b1.at[0], y, at_y)
     first_b = first(gat_b, sem_b1.at[1], z, at_z)
-    gat_a[place(0)] = flat[:, :lanes_a].astype(bf16)
+    gat_a[place(0)] = flat[:, :gat_a.shape[2]].astype(bf16)
     first_a.start(near + far)
-    gat_b[place(0)] = flat[:, lanes_a:].astype(bf16)
+    gat_b[place(0)] = flat[:, lanes_a:lanes_a + gat_b.shape[2]].astype(bf16)
     first_b.start(near + far)
 
     out = lax.broadcasted_iota(jnp.int32, (block_rows // 2, n // 2 * ROWS), 0)
     src = lax.broadcasted_iota(jnp.int32, (block_rows // 2, n // 2 * ROWS), 1)
     dense = jnp.where(src == out // per * ROWS + lax.rem(out, per), 1.0, 0.0).astype(bf16)
+    group_rows = n // 2 * ROWS
+    out = lax.broadcasted_iota(jnp.int32, (block_rows, per * group_rows), 0)
+    src = lax.broadcasted_iota(jnp.int32, (block_rows, per * group_rows), 1)
+    k, out = out // (block_rows // 2), lax.rem(out, block_rows // 2)
+    unfold = jnp.where(src == lax.rem(out, per) * group_rows + out // per * ROWS + per + k, 1.0, 0.0).astype(bf16)
 
     def packed(gat, part):
         piece = gat[part * (n // 2):(part + 1) * (n // 2)]
-        return dot(dense, piece.reshape(n // 2 * ROWS, gat.shape[2]), (1, 0))
+        piece = piece.reshape(group_rows, gat.shape[2])
+        folded = jnp.concatenate([piece[:, 128 * q:128 * (q + 1)] for q in range(per)], axis=0)
+        tails = dot(unfold, folded, (1, 0))
+        return jnp.concatenate([dot(dense, piece, (1, 0)), tails[:block_rows // 2], tails[block_rows // 2:]], axis=1)
 
     spread_a = Spread(rows_a, sem_b2.at[0], nz, z, at_z)
     spread_b = Spread(rows_b, sem_b2.at[1], ny, y, at_y)
@@ -272,9 +285,17 @@
         used[0, c * n * n:(c + 1) * n * n] = gates * back_grad * slope
         used[1, c * n * n:(c + 1) * n * n] = gates * value
 
+    full = half // 128
+
     def terms(rows, weights, send):
         result = dot(rows[:, :hidden].astype(bf16), weights, (1, 0))
-        send[...] = result.reshape(send.shape).astype(bf16)
+        result = result.reshape(n, CAP, n, half)
+        for c in range(CAP):
+            for t in range(full):
+                send[:, c * full + t] = result[:, c, :, 128 * t:128 * (t + 1)].astype(bf16)
+        tails = [result[:, c, :, 128 * full:] for c in range(CAP)]
+        tails.append(jnp.zeros((n, n, 128 - CAP * (half - 128 * full)), f32))
+        send[:, CAP * full] = jnp.concatenate(tails, axis=2).astype(bf16)
 
     def first_sum(send, recv, sems, me, device_of):
         return Exchange(lambda d: send.at[place(d)], lambda d: recv.at[d], lambda d: recv.at[d], sems, n, me, device_of)
@@ -308,24 +329,29 @@
         grad2[:, first_lane:first_lane + width] = product[128:128 + hidden, :width]
 
     quarter = half // 2
-    tiles = fold.shape[0]
+    tiles = quarter // 128
+    tail = quarter - 128 * tiles
+    half_tail = half - 128 * full
 
     def second(exchange, send_first, recv, send, again, sems, me, device_of):
         exchange.wait_recv(far_first(n)[::-1])
         total = send_first[place(0)].astype(f32)
         for d in range(1, n):
             total = total + recv[d].astype(f32)
-        total = total.reshape(CAP * n, half)
-        for h in (0, 1):
-            piece = total[:, h * quarter:(h + 1) * quarter]
-            for t in range(tiles):
-                width = min(128, quarter - 128 * t)
-                fold[t, h * CAP * n:(h + 1) * CAP * n, :width] = piece[:, 128 * t:128 * t + width]
-        for i in range(n):
-            for t in range(tiles):
-                width = min(128, quarter - 128 * t)
-                send[i, :per, 128 * t:128 * t + width] = fold[t, pl.ds(i, per, stride=n), :][:, :width]
-        again_sum = Exchange(lambda d: send.at[place(d)], lambda d: again.at[d], lambda d: again.at[d], sems, n, me, device_of)
+        tails = []
+        for c in range(CAP):
+            whole = [total[c * full + t] for t in range(full)]
+            whole.append(total[CAP * full][:, c * half_tail:(c + 1) * half_tail])
+            whole = jnp.concatenate(whole, axis=1)
+            for h in (0, 1):
+                for t in range(tiles):
+                    start = h * quarter + 128 * t
+                    send[t, pl.ds(h * CAP + c, n, stride=ROWS), :] = whole[:, start:start + 128]
+                tails.append((h * CAP + c, whole[:, h * quarter + 128 * tiles:(h + 1) * quarter]))
+        tails = [piece for _, piece in sorted(tails, key=lambda item: item[0])]
+        tails.append(jnp.zeros((n, 128 - per * tail), f32))
+        send[0, pl.ds(per, n, stride=ROWS), :] = jnp.concatenate(tails, axis=1)
+        again_sum = Exchange(lambda d: send.at[:, pl.ds(place(d) * ROWS, ROWS)], lambda d: again.at[d], lambda d: again.at[d], sems, n, me, device_of)
         again_sum.start(far_first(n))
         return again_sum
 
@@ -335,9 +361,12 @@
     quarter_chunks = ne // 4
     for which, exchange, send, again in ((0, again_a, send_2a, recv_2a), (1, again_b, send_2b, recv_2b)):
         exchange.wait_recv(far_first(n)[::-1])
-        total = send[place(0)]
+        total = send[:, place(0) * ROWS:(place(0) + 1) * ROWS]
         for d in range(1, n):
             total = total + again[d]
+        tails = [total[0][per:per + 1, q * tail:(q + 1) * tail] for q in range(per)]
+        tails.append(jnp.zeros((ROWS - per, tail), f32))
+        total = jnp.concatenate([total[t] for t in range(tiles)] + [jnp.concatenate(tails, axis=0)], axis=1)
         for i in range(quarter_chunks):
             send_e[which * quarter_chunks + i] = total[:, i * chunk:(i + 1) * chunk].astype(bf16)
 
@@ -391,8 +420,8 @@
         vmem((ne, ROWS, chunk), bf16),
         vmem((ne, ROWS, chunk), bf16),
         vmem((ROWS, lanes_a + lanes_b), f32),
-        vmem((n, ROWS, lanes_a), bf16),
-        vmem((n, ROWS, lanes_b), bf16),
+        vmem((n, ROWS, lanes_a - 128 * (ROWS - per)), bf16),
+        vmem((n, ROWS, lanes_b - 128 * (ROWS - per)), bf16),
         vmem((n, 2, part_rows // step_rows, step_rows, lanes_a), bf16),
         vmem((n, 2, part_rows // step_rows, step_rows, lanes_b), bf16),
         vmem((2, n * n * per, 128), f32),
@@ -400,15 +429,14 @@
         vmem((2, CAP * n * n, 128), f32),
         vmem((2, n * n * per, 128), f32),
         vmem((2, n * n * per, 128), f32),
-        vmem((n, CAP, n, half), bf16),
-        vmem((n, CAP, n, half), bf16),
-        vmem((n, CAP, n, half), bf16),
-        vmem((n, CAP, n, half), bf16),
-        vmem((math.ceil(half // 2 / 128), per * n, 128), f32),
-        vmem((n, ROWS, half // 2), f32),
-        vmem((n, ROWS, half // 2), f32),
-        vmem((n, ROWS, half // 2), f32),
-        vmem((n, ROWS, half // 2), f32),
+        vmem((n, CAP * (half // 128) + 1, n, 128), bf16),
+        vmem((n, CAP * (half // 128) + 1, n, 128), bf16),
+        vmem((n, CAP * (half // 128) + 1, n, 128), bf16),
+        vmem((n, CAP * (half // 128) + 1, n, 128), bf16),
+        vmem((half // 2 // 128, n * ROWS, 128), f32),
+        vmem((half // 2 // 128, n * ROWS, 128), f32),
+        vmem((n, half // 2 // 128, ROWS, 128), f32),
+        vmem((n, half // 2 // 128, ROWS, 128), f32),
         vmem((ne // 2, ROWS, chunk), bf16),
         vmem((ne, ROWS, chunk), bf16),
         dma((7,)),

time: 73.5 us -> 72.2 us (0.982)
  Pallas kernels: 70.3 us -> 69 us
    pallas_call x1, Pallas kernels: 70.3 us -> 69 us  [local(): pl.pallas_call(functools.partial(kernel, cfg), out_shape=(jax.ShapeDtypeS...]
where the time goes in v3:
time: 72.2 us; the launch traced here: 72 us
  Pallas kernels  69 us (96%)
  local copies, waits for them, and re-layouts  2.39 us (3%)
    pallas_call x1, Pallas kernels, local(): pl.pallas_call(functools.partial(kernel, cfg), out_shape=(jax.ShapeDtypeS...  69 us
    unnamed x3, local copies, waits for them, and re-layouts  2.39 us

profile of v3, /device:TPU:1, one launch (start us, length us, event | category | flops | bytes accessed | tf_op | source)
XLA Modules:
  0.0 72.0 jit_solution(11188018076864122435)
XLA Ops:
  0.6 69.0 %moe_backward.1 = (bf16[24,130]{1,0:T(8,128)(2,1)S(1)}, f32[96,2080]{1,0:T(8,128)S(1)}, f32[96,2080]{1,0:T(8,128)S(1)}) custom-call(bf16[24,130]{1,0:T(8,128)(2,1)} %tok_hbm.1, bf16[24,130]{1,0:T(8,128)(2,1)} %og_hbm.1, bf16[1,24]{1,0:T(2,128)(2,1)} %bitcast.15, s32[1,24]{1,0:T(1,128)} %bitcast.16, s32[1,24]{1,0:T(1,128)} %bitcast.17, ...), custom_call_target="tpu_custom_call" | custom-call | tf_op jit(solution)/shard_map/moe_backward/pallas_call | solution.py:453
  69.7 0.6 copy.13
  70.3 0.9 %copy.14 = f32[1,2080,96]{1,2,0:T(8,128)} copy(f32[1,2080,96]{1,2,0:T(8,128)S(1)} %bitcast.12) | data formatting | bytes 1597440
  71.2 0.9 %copy.15 = f32[1,96,2080]{2,1,0:T(8,128)} copy(f32[1,96,2080]{2,1,0:T(8,128)S(1)} %bitcast.11) | data formatting | bytes 1597440

commit v4 on v3

--- a/solution.py
+++ b/solution.py
@@ -72,7 +72,7 @@
         self.sent = []
         if n > 4:
             self.first = {0: (-2, 2), 1: (2, -2), 2: (-1, 1), 3: (1, -1)}
-            self.second = {4: (-3, 1), 5: (3, -1), 6: (4, 2), 7: (4, -2)}
+            self.second = {4: (-3, 1), 5: (3, -1), 6: (4, 1), 7: (4, -2)}
         else:
             self.first = {0: (1, 1)}
             self.second = {}
@@ -108,13 +108,21 @@
         if self.second:
             for index, through, across in ((0, 4, 6), (1, 5, 7)):
                 self.receive(index, part)
-                if part == index:
+                if part == index == 1:
                     self.send(across, part)
                 self.send(through, part)
 
-    def finish(self, part):
+    def third(self):
+        if self.second:
+            self.receive(4, 0)
+            self.send(6, 0)
+
+    def finish_first(self, part):
         for index in self.first:
             self.receive(index, part)
+
+    def finish(self, part):
+        self.finish_first(part)
         if self.second:
             for index in (4, 5, 6 + part):
                 self.receive(index, part)
@@ -256,21 +264,38 @@
     for part in (0, 1):
         for spread in (spread_a, spread_b):
             spread.forward(part)
+    for spread in (spread_a, spread_b):
+        spread.third()
+    def block_of(i):
+        return (i - 1 + n // 2 - 1) % n
+
+    early = [i for i in range(n) if n > 4 and 1 <= block_of(i) <= n - 3]
+    late = [i for i in range(n) if i not in early]
+
+    def products(places, count):
+        for hid, rows, weights in ((hid_a, rows_a, wa), (hid_b, rows_b, wb)):
+            width = rows.shape[-1]
+            if count:
+                block = rows[1:1 + count]
+            else:
+                block = jnp.concatenate([rows[block_of(i):block_of(i) + 1] for i in places], axis=0)
+            product = dot(block.reshape(len(places) * block_rows, width), weights[...], (1, 1))
+            for k, i in enumerate(sorted(places, key=block_of) if count else places):
+                here = product[k * block_rows:(k + 1) * block_rows]
+                hid[0, i * block_rows:(i + 1) * block_rows] = here[:, :128]
+                hid[1, i * block_rows:(i + 1) * block_rows] = here[:, 128:]
+
+    if early:
+        for part in (0, 1):
+            for spread in (spread_a, spread_b):
+                spread.finish_first(part)
+        products(early, len(early))
     for part in (0, 1):
         for spread in (spread_a, spread_b):
             spread.finish(part)
-
-    def block_of(i):
-        return (i - 1 + n // 2 - 1) % n
-
+    products(late, 0)
     all_a = rows_a[...].reshape(n * block_rows, lanes_a)
     all_b = rows_b[...].reshape(n * block_rows, lanes_b)
-    for hid, rows, weights in ((hid_a, all_a, wa), (hid_b, all_b, wb)):
-        product = dot(rows, weights[...], (1, 1))
-        for i in range(n):
-            here = product[block_of(i) * block_rows:(block_of(i) + 1) * block_rows]
-            hid[0, i * block_rows:(i + 1) * block_rows] = here[:, :128]
-            hid[1, i * block_rows:(i + 1) * block_rows] = here[:, 128:]
 
     def gathered(which, q):
         return jnp.concatenate([

time: 72.2 us -> 71.2 us (0.986)
  Pallas kernels: 69 us -> 67.9 us
    pallas_call x1, Pallas kernels: 69 us -> 67.9 us  [local(): pl.pallas_call(functools.partial(kernel, cfg), out_shape=(jax.ShapeDtypeS...]
where the time goes in v4:
time: 71.2 us; the launch traced here: 71 us
  Pallas kernels  67.9 us (95%)
  local copies, waits for them, and re-layouts  2.39 us (3%)
    pallas_call x1, Pallas kernels, local(): pl.pallas_call(functools.partial(kernel, cfg), out_shape=(jax.ShapeDtypeS...  67.9 us
    unnamed x3, local copies, waits for them, and re-layouts  2.39 us

profile of v4, /device:TPU:1, one launch (start us, length us, event | category | flops | bytes accessed | tf_op | source)
XLA Modules:
  0.0 71.0 jit_solution(1885078459972594945)
XLA Ops:
  0.6 67.9 %moe_backward.1 = (bf16[24,130]{1,0:T(8,128)(2,1)S(1)}, f32[96,2080]{1,0:T(8,128)S(1)}, f32[96,2080]{1,0:T(8,128)S(1)}) custom-call(bf16[24,130]{1,0:T(8,128)(2,1)} %tok_hbm.1, bf16[24,130]{1,0:T(8,128)(2,1)} %og_hbm.1, bf16[1,24]{1,0:T(2,128)(2,1)} %bitcast.15, s32[1,24]{1,0:T(1,128)} %bitcast.16, s32[1,24]{1,0:T(1,128)} %bitcast.17, ...), custom_call_target="tpu_custom_call" | custom-call | tf_op jit(solution)/shard_map/moe_backward/pallas_call | solution.py:478
  68.6 0.6 copy.13
  69.2 0.9 %copy.14 = f32[1,2080,96]{1,2,0:T(8,128)} copy(f32[1,2080,96]{1,2,0:T(8,128)S(1)} %bitcast.12) | data formatting | bytes 1597440
  70.1 0.9 %copy.15 = f32[1,96,2080]{2,1,0:T(8,128)} copy(f32[1,96,2080]{2,1,0:T(8,128)S(1)} %bitcast.11) | data formatting | bytes 1597440
